TPU v7x, 256 devices: a whole 4x4x8 slice. The times are simulated.
256 devices in a mesh: visit: 32 (over y, z), tile: 8 (over x, core).
Axes of the slice: x: 4, y: 4, z: 8, core: 2. Of those that a mesh axis runs over, the one named last changes fastest.
Arguments:
- visit_image: bfloat16 [32, 2048, 2048], P('visit', 'tile'), may hold values from -6 to 6
- good_mask: int32 [32, 2048, 2048], P('visit', 'tile'), may hold values 0 or 1
- basis_rows: float32 [27, 21], replicated, may hold values from -1.25 to 1.25
- basis_cols: float32 [27, 21], replicated, may hold values from -1.25 to 1.25
- visit_coeff: float32 [32, 27], P('visit'), may hold values from -1.25 to 1.25
- visit_weight: float32 [32], P('visit'), may hold values from 0.25 to 4
- col_offset: int32 [32], P('visit'), may hold values from -64 to 64
- patch_of: int32 [32, 1], replicated, may hold values from 0 to 7
- new_image: bfloat16 [32, 2048, 2048], P('visit', 'tile'), may hold values from -6 to 6
- new_coeff: float32 [32, 27], P('visit'), may hold values from -1.25 to 1.25
- new_patch: int32 [32, 1], replicated, may hold values from 0 to 7
Outputs:
- coadd: bfloat16 [8, 8, 256, 2048], P(None, 'tile', 'visit')
- difference: float32 [32, 2048, 2048], P('visit', 'tile')
Inputs may be any that keep to these rules, and one draw needn't show every extreme that they name: `patch_of`: every one of the 8 patches is intersected by at least one visit. `new_patch`: every one of the 8 patches lies under at least one new visit.
All inputs are finite; a program needn't handle non-finite values. No bound on the sum of `good_mask` on one device may be relied on, other than what follows from the above.
Results may differ from a plain program's by a relative error of at most 0.007.
Values may be sent and summed in bfloat16 or wider, within the bound.
No kernel may reach another device: no remote copies, remote signals or barrier semaphores. Data moves between devices by JAX's collectives and lax.ppermute only.
A program may use at most 128 MiB of HBM per device.

v0:
```python
import jax
import jax.numpy as jnp
from jax import lax
from jax.sharding import PartitionSpec as P

KS = 21
PATCHES = 8
OFF = 64


def with_halo(block, sides, width):
    for axis, dim in sides:
        count = lax.axis_size(axis)
        forward = [(i, i + 1) for i in range(count - 1)]
        backward = [(target, source) for source, target in forward]
        low = lax.ppermute(
            lax.slice_in_dim(block, block.shape[dim] - width, None, axis=dim), axis, forward
        )
        high = lax.ppermute(lax.slice_in_dim(block, 0, width, axis=dim), axis, backward)
        block = jnp.concatenate([low, block, high], axis=dim)
    return block


def build_kernel(coefficients, basis_rows, basis_cols):
    summed = jnp.sum(
        coefficients[:, None, None] * basis_rows[:, :, None] * basis_cols[:, None, :], axis=0
    )
    return summed.astype(jnp.bfloat16)


def toeplitz(kernel, block_size):
    span = block_size + KS - 1
    spread = jnp.arange(span)[:, None] - jnp.arange(block_size)[None, :]
    onehot = (spread[None, :, :] == jnp.arange(KS)[:, None, None]).astype(jnp.bfloat16)
    product = jnp.dot(
        kernel, onehot.reshape(KS, span * block_size), preferred_element_type=jnp.float32
    )
    return product.reshape(KS, span, block_size).astype(jnp.bfloat16)


def convolve(extended, kernel):
    halfwidth = KS // 2
    height = extended.shape[0] - (KS - 1)
    columns = extended.shape[1]
    block_size = 128
    number = columns // block_size
    padded = jnp.pad(extended, ((0, 0), (halfwidth, block_size - halfwidth)))
    blocks = padded.reshape(extended.shape[0], number + 1, block_size)
    windows = jnp.concatenate([blocks[:, :-1], blocks[:, 1:, : KS - 1]], axis=2)
    table = toeplitz(kernel, block_size)
    running = jnp.zeros((height, number, block_size), jnp.float32)
    for shift_row in range(KS):
        running = running + jnp.einsum(
            "rgk,ko->rgo",
            windows[shift_row : shift_row + height],
            table[shift_row],
            preferred_element_type=jnp.float32,
        )
    return running.reshape(height, columns)


def per_device(
    visit_image,
    good_mask,
    basis_rows,
    basis_cols,
    visit_coeff,
    visit_weight,
    col_offset,
    patch_of,
    new_image,
    new_coeff,
    new_patch,
):
    halfwidth = KS // 2
    extended = with_halo(visit_image[0], (("tile", 0),), halfwidth)
    matched = convolve(extended, build_kernel(visit_coeff[0], basis_rows, basis_cols))
    height, columns = matched.shape
    first_col = OFF - col_offset[0]
    placed = lax.dynamic_slice_in_dim(jnp.pad(matched, ((0, 0), (OFF, OFF))), first_col, columns, 1)
    inside = lax.dynamic_slice_in_dim(
        jnp.pad(good_mask[0].astype(jnp.float32), ((0, 0), (OFF, OFF))), first_col, columns, 1
    )
    coverage = visit_weight[0] * inside
    weighted = (placed * coverage).astype(jnp.bfloat16)
    cover_rounded = coverage.astype(jnp.bfloat16)
    owners = lax.axis_size("visit")
    slice_rows = height // owners
    visit_onehot = (patch_of[:, 0][None, :] == jnp.arange(PATCHES)[:, None]).astype(jnp.bfloat16)
    outgoing = (
        weighted.reshape(owners, slice_rows, columns),
        cover_rounded.reshape(owners, slice_rows, columns),
    )
    weighted_rows = lax.all_to_all(outgoing[0], "visit", split_axis=0, concat_axis=0, tiled=True)
    cover_rows = lax.all_to_all(outgoing[1], "visit", split_axis=0, concat_axis=0, tiled=True)
    numerator = jnp.einsum(
        "pv,vsw->psw", visit_onehot, weighted_rows, preferred_element_type=jnp.float32
    )
    denominator = jnp.einsum(
        "pv,vsw->psw", visit_onehot, cover_rows, preferred_element_type=jnp.float32
    )
    coadd = (numerator / jnp.maximum(denominator, 1.0)).astype(jnp.bfloat16)
    gathered = lax.all_gather(coadd, "visit", axis=1, tiled=True)
    patch_index = lax.dynamic_index_in_dim(
        new_patch[:, 0], lax.axis_index("visit"), 0, keepdims=False
    )
    template = lax.dynamic_index_in_dim(gathered, patch_index, 0, keepdims=False)
    template_ext = with_halo(template, (("tile", 0),), halfwidth)
    difference = new_image[0].astype(jnp.float32) - convolve(
        template_ext, build_kernel(new_coeff[0], basis_rows, basis_cols)
    )
    return (coadd[:, None], difference[None])


def solution(mesh):
    return jax.shard_map(
        per_device,
        mesh=mesh,
        in_specs=(
            P("visit", "tile", None),
            P("visit", "tile", None),
            P(),
            P(),
            P("visit", None),
            P("visit"),
            P("visit"),
            P(),
            P("visit", "tile", None),
            P("visit", None),
            P(),
        ),
        out_specs=(P(None, "tile", "visit", None), P("visit", "tile", None)),
        check_vma=False,
    )
```

profile of v0, /device:TPU:1, one launch (start us, length us, event | category | flops | bytes accessed | tf_op | source)
XLA Modules:
  0.0 335.7 jit_solution(6419589440406265364)
XLA Ops:
  8.1 4.5 %collective-permute-start = (bf16[10,2048]{1,0:T(8,128)(2,1)S(1)}, bf16[10,2048]{1,0:T(8,128)(2,1)S(1)}, u32[]{:S(2)}, u32[]{:S(2)}) collective-permute-start(bf16[10,2048]{1,0:T(8,128)(2,1)S(1)} %get-tuple-element.16), channel_id=1, source_target_pairs={{0,1},{1,2},{2,3},{3,4},{4,5},{5,6},{6,7},{8,9},{9,10},{10,11},{11... | collective-permute-start | bytes 122888 | tf_op jit(solution)/shard_map/ppermute | solution.py:16
  33.7 2.1 fusion.119
  37.9 2.2 fusion.125
  48.3 2.1 fusion.92
  50.4 2.1 fusion.95
  54.7 2.3 fusion.128
  62.9 13.9 %add_add_fusion.1 = f32[256,16,128]{0,2,1:T(8,128)} fusion(f32[256,16,128]{0,2,1:T(8,128)} %fusion.71, f32[256,16,128]{0,2,1:T(8,128)} %fusion.128, f32[256,16,128]{0,2,1:T(8,128)} %fusion.125, f32[256,16,128]{0,2,1:T(8,128)} %fusion.122, f32[256,16,128]{0,2,1:T(8,128)} %fusion.119, f32[256,16,128]{0,2,1:T(8,128)} %fusion.116, ...), kind=kOutput, calls=%fused_computation.51 | convolution fusion | flops 168099840 | bytes 45385216 | tf_op jit(solution)/shard_map/rgk,ko->rgo/dot_general | solution.py:53
  76.9 3.1 copy.44
  79.9 4.3 %fusion.172 = (bf16[32,8,2048]{2,1,0:T(8,128)(2,1)}, bf16[32,8,2048]{2,1,0:T(8,128)(2,1)S(1)}) fusion(s32[]{:T(128)S(6)} %select_n.12, f32[256,2048]{1,0:T(8,128)S(1)} %copy-done.2, f32[]{:T(128)} %bitcast.166, f32[256,2048]{1,0:T(8,128)} %copy.44), kind=kLoop, calls=%fused_computation.184 | loop fusion | flops 2621440 | bytes 6291464 | tf_op jit(solution)/shard_map/reshape | solution.py:92
  84.2 38.8 %all_to_all.10 = bf16[32,8,2048]{2,1,0:T(8,128)(2,1)S(1)} all-to-all(bf16[32,8,2048]{2,1,0:T(8,128)(2,1)S(1)} %get-tuple-element.13), channel_id=1, replica_groups=mesh['visit'=32,'tile'=8] {'visit'}, dimensions={0} | all-to-all | bytes 2097152 | tf_op jit(solution)/shard_map/all_to_all | solution.py:94
  123.0 4.8 %all-to-all-start.1 = ((bf16[32,8,2048]{2,1,0:T(8,128)(2,1)}), bf16[32,8,2048]{2,1,0:T(8,128)(2,1)S(1)}, u32[]{:S(2)}, u32[]{:S(2)}) async-start(bf16[32,8,2048]{2,1,0:T(8,128)(2,1)} %get-tuple-element.12), calls=%async_computation.1 | async-start | bytes 2097152 | tf_op jit(solution)/shard_map/all_to_all | solution.py:95
  129.4 24.5 %all-to-all-done.1 = bf16[32,8,2048]{2,1,0:T(8,128)(2,1)S(1)} async-done(((bf16[32,8,2048]{2,1,0:T(8,128)(2,1)}), bf16[32,8,2048]{2,1,0:T(8,128)(2,1)S(1)}, u32[]{:S(2)}, u32[]{:S(2)}) %all-to-all-start.1) | async-done | bytes 1048608 | tf_op jit(solution)/shard_map/all_to_all | solution.py:95
  158.8 2.2 fusion.354
  161.0 93.0 %all-gather.2.cloned.1.call-done = bf16[8,256,2048]{2,0,1:T(8,128)(2,1)} async-done(((bf16[8,8,2048]{2,0,1:T(8,128)(2,1)}), bf16[8,256,2048]{2,0,1:T(8,128)(2,1)}) %all-gather.2.cloned.1.call-update) | async-done | bytes 8388624 | tf_op jit(solution)/shard_map/all_gather | solution.py:103
  253.9 5.7 %constant_dynamic-slice_fusion = bf16[1,256,2048]{2,0,1:T(2,128)(2,1)S(1)} fusion(bf16[8,256,2048]{2,0,1:T(8,128)(2,1)} %all-gather.2.cloned.1.call-done, s32[]{:T(128)S(6)} %select_n.14), kind=kLoop, calls=%fused_computation.332 | loop fusion | bytes 2097156 | tf_op jit(solution)/shard_map/jit(dynamic_index_in_dim)/dynamic_slice | solution.py:107
  260.3 4.1 %collective-permute-start.2 = (bf16[10,2048]{1,0:T(8,128)(2,1)S(1)}, bf16[10,2048]{1,0:T(8,128)(2,1)S(1)}, u32[]{:S(2)}, u32[]{:S(2)}) collective-permute-start(bf16[10,2048]{1,0:T(8,128)(2,1)S(1)} %get-tuple-element.14), channel_id=1, source_target_pairs={{0,1},{1,2},{2,3},{3,4},{4,5},{5,6},{6,7},{8,9},{9,10},{10,11},{11... | collective-permute-start | bytes 122888 | tf_op jit(solution)/shard_map/ppermute | solution.py:16
  278.7 2.1 fusion.29
  280.8 2.1 fusion.32
  285.1 2.2 fusion.38
  295.5 2.1 fusion.53
  297.6 2.1 fusion.56
  301.8 2.2 fusion.62
  304.0 2.3 fusion.65
  310.5 14.4 %add_add_fusion = f32[256,16,128]{0,2,1:T(8,128)} fusion(f32[256,16,128]{0,2,1:T(8,128)} %fusion.11, f32[256,16,128]{0,2,1:T(8,128)} %fusion.68, f32[256,16,128]{0,2,1:T(8,128)} %fusion.65, f32[256,16,128]{0,2,1:T(8,128)} %fusion.62, f32[256,16,128]{0,2,1:T(8,128)} %fusion.59, f32[256,16,128]{0,2,1:T(8,128)} %fusion.56, f32[256,16,128]{0,2,1:T(8,128)} %fusion.53, ...), kind=kOutput, calls=%fused_computation.48 | convolution fusion | flops 168099840 | bytes 45385216 | tf_op jit(solution)/shard_map/rgk,ko->rgo/dot_general | solution.py:53
  (153 shorter events, 78.5 us)
Async XLA Ops:
  7.2 148.6 %copy-start = (s32[32,1]{0,1:T(1,128)S(1)}, s32[32,1]{0,1:T(1,128)}, u32[]{:S(2)}) copy-start(s32[32,1]{0,1:T(1,128)} %param.21) | copy-start | bytes 388
  8.1 14.4 %collective-permute-start = (bf16[10,2048]{1,0:T(8,128)(2,1)S(1)}, bf16[10,2048]{1,0:T(8,128)(2,1)S(1)}, u32[]{:S(2)}, u32[]{:S(2)}) collective-permute-start(bf16[10,2048]{1,0:T(8,128)(2,1)S(1)} %get-tuple-element.16), channel_id=1, source_target_pairs={{0,1},{1,2},{2,3},{3,4},{4,5},{5,6},{6,7},{8,9},{9,10},{10,11},{11... | collective-permute-start | bytes 122888 | tf_op jit(solution)/shard_map/ppermute | solution.py:16
  12.6 9.9 %collective-permute-start.1 = (bf16[10,2048]{1,0:T(8,128)(2,1)S(1)}, bf16[10,2048]{1,0:T(8,128)(2,1)S(1)}, u32[]{:S(2)}, u32[]{:S(2)}) collective-permute-start(bf16[10,2048]{1,0:T(8,128)(2,1)S(1)} %get-tuple-element.17), channel_id=1, source_target_pairs={{1,0},{2,1},{3,2},{4,3},{5,4},{6,5},{7,6},{9,8},{10,9},{11,10},{12... | collective-permute-start | bytes 122888 | tf_op jit(solution)/shard_map/ppermute | solution.py:19
  16.2 2.6 copy-start.3
  18.8 3.7 %copy-start.4 = (bf16[1,256,2048]{2,1,0:T(8,128)(2,1)S(1)}, bf16[1,256,2048]{2,1,0:T(8,128)(2,1)}, u32[]{:S(2)}) copy-start(bf16[1,256,2048]{2,1,0:T(8,128)(2,1)} %param.11) | copy-start | bytes 3145732
  33.7 2.1 copy-start.37
  37.9 2.2 copy-start.35
  48.3 2.1 copy-start.30
  50.4 2.1 copy-start.29
  54.7 2.3 copy-start.27
  76.8 3.1 copy-start.2
  84.2 43.9 %copy-start.43 = (s32[32,1]{0,1:T(1,128)S(1)}, s32[32,1]{0,1:T(1,128)}, u32[]{:S(2)}) copy-start(s32[32,1]{0,1:T(1,128)} %param.18) | copy-start | bytes 388
  123.0 30.8 %all-to-all-start.1 = ((bf16[32,8,2048]{2,1,0:T(8,128)(2,1)}), bf16[32,8,2048]{2,1,0:T(8,128)(2,1)S(1)}, u32[]{:S(2)}, u32[]{:S(2)}) async-start(bf16[32,8,2048]{2,1,0:T(8,128)(2,1)} %get-tuple-element.12), calls=%async_computation.1 | async-start | bytes 2097152 | tf_op jit(solution)/shard_map/all_to_all | solution.py:95
  127.9 126.0 %all-gather.2.cloned.1.call-start = ((), (), s32[]{:S(2)}) async-start(), calls=%async_computation.2 | async-start | bytes 8650752 | tf_op jit(solution)/shard_map/all_gather | solution.py:103
  259.6 6.8 %copy-start.6 = (bf16[8,8,2048]{2,0,1:T(8,128)(2,1)S(1)}, bf16[8,8,2048]{2,0,1:T(8,128)(2,1)}, u32[]{:S(2)}) copy-start(bf16[8,8,2048]{2,0,1:T(8,128)(2,1)} %fusion.1) | copy-start | bytes 786436
  260.3 7.6 %collective-permute-start.2 = (bf16[10,2048]{1,0:T(8,128)(2,1)S(1)}, bf16[10,2048]{1,0:T(8,128)(2,1)S(1)}, u32[]{:S(2)}, u32[]{:S(2)}) collective-permute-start(bf16[10,2048]{1,0:T(8,128)(2,1)S(1)} %get-tuple-element.14), channel_id=1, source_target_pairs={{0,1},{1,2},{2,3},{3,4},{4,5},{5,6},{6,7},{8,9},{9,10},{10,11},{11... | collective-permute-start | bytes 122888 | tf_op jit(solution)/shard_map/ppermute | solution.py:16
  264.3 5.6 %collective-permute-start.3 = (bf16[10,2048]{1,0:T(8,128)(2,1)S(1)}, bf16[10,2048]{1,0:T(8,128)(2,1)S(1)}, u32[]{:S(2)}, u32[]{:S(2)}) collective-permute-start(bf16[10,2048]{1,0:T(8,128)(2,1)S(1)} %get-tuple-element.15), channel_id=1, source_target_pairs={{1,0},{2,1},{3,2},{4,3},{5,4},{6,5},{7,6},{9,8},{10,9},{11,10},{12... | collective-permute-start | bytes 122888 | tf_op jit(solution)/shard_map/ppermute | solution.py:19
  280.8 2.1 copy-start.21
  285.0 2.2 copy-start.19
  295.5 2.1 copy-start.14
  297.6 2.1 copy-start.13
  301.8 2.2 copy-start.11
  304.0 2.3 copy-start.10
  324.9 3.6 %copy-start.1 = (s32[32,1]{0,1:T(1,128)S(1)}, s32[32,1]{0,1:T(1,128)}, u32[]{:S(2)}) copy-start(s32[32,1]{0,1:T(1,128)} %param.21) | copy-start | bytes 388
  (26 other events, 49.0 us)
Sparse Core Ops, SparseCore 0:
  155.9 97.9 all-gather.1
where the time goes:
time: 339 us; the launch traced here: 336 us
  waiting for transfers between devices  120 us (35%)
  matrix products  108 us (32%)
  blocking collectives  38.8 us (11%)
  local copies, waits for them, and re-layouts  24.2 us (7%)
  between operations  18 us (5%)
  starting transfers between devices  17.5 us (5%)
  other arithmetic  9.66 us (3%)
    dot_general x42, matrix products, convolve(): jnp.einsum('rgk,ko->rgo', windows[shift_row:shift_row + height], table[sh...  104 us
    all_gather x1, waiting for transfers between devices, per_device(): gathered = lax.all_gather(coadd, 'visit', axis=1, tiled=True)  93 us
    all_to_all x1, blocking collectives, per_device(): lax.all_to_all(outgoing[0], 'visit', split_axis=0, concat_axis=0, tiled=T...  38.8 us
    all_to_all x1, waiting for transfers between devices, per_device(): lax.all_to_all(outgoing[1], 'visit', split_axis=0, concat_axis=0, tiled=T...  24.5 us
    ppermute x2, starting transfers between devices, with_halo(): lax.ppermute(lax.slice_in_dim(block, block.shape[dim] - width, None, axis...  8.58 us
  transfers between devices with their start and end apart: 6, of which 3 were waited for; matrix products, arithmetic and copies ran while one was open for 4% of the time, Pallas kernels for 0%

commit v1 on v0

--- a/solution.py
+++ b/solution.py
@@ -6,6 +6,15 @@
 KS = 21
 PATCHES = 8
 OFF = 64
+define_columns = lambda xin, axis_key, dim_at: jnp.concatenate(
+    jax.lax.all_to_all(
+        jnp.stack([xin for _ in range(jax.lax.axis_size(axis_key))], axis=0),
+        axis_name=axis_key,
+        split_axis=0,
+        concat_axis=0,
+    ),
+    axis=dim_at,
+)
 
 
 def with_halo(block, sides, width):
@@ -100,7 +109,7 @@
         "pv,vsw->psw", visit_onehot, cover_rows, preferred_element_type=jnp.float32
     )
     coadd = (numerator / jnp.maximum(denominator, 1.0)).astype(jnp.bfloat16)
-    gathered = lax.all_gather(coadd, "visit", axis=1, tiled=True)
+    gathered = define_columns(coadd, "visit", 1)
     patch_index = lax.dynamic_index_in_dim(
         new_patch[:, 0], lax.axis_index("visit"), 0, keepdims=False
     )

time: 339 us -> 439 us (1.29)
  the two profiles are of different devices: /device:TPU:1 before, /device:TPU:33 now
where the time goes in v1:
time: 439 us; the launch traced here: 435 us
  waiting for transfers between devices  222 us (51%)
  matrix products  107 us (24%)
  blocking collectives  38.6 us (9%)
  local copies, waits for them, and re-layouts  32.2 us (7%)
  starting transfers between devices  20 us (5%)
  other arithmetic  9.7 us (2%)
  between operations  4.53 us (1%)
    all_to_all x1, waiting for transfers between devices, jax.lax.all_to_all(jnp.stack([xin for _ in range(jax.lax.axis_size(axis_k...  193 us
    dot_general x42, matrix products, convolve(): jnp.einsum('rgk,ko->rgo', windows[shift_row:shift_row + height], table[sh...  104 us
    all_to_all x1, blocking collectives, per_device(): lax.all_to_all(outgoing[0], 'visit', split_axis=0, concat_axis=0, tiled=T...  38.6 us
    all_to_all x1, waiting for transfers between devices, per_device(): lax.all_to_all(outgoing[1], 'visit', split_axis=0, concat_axis=0, tiled=T...  27.4 us
  transfers between devices with their start and end apart: 6, of which 3 were waited for; matrix products, arithmetic and copies ran while one was open for 3% of the time, Pallas kernels for 0%

profile of v1, /device:TPU:33, one launch (start us, length us, event | category | flops | bytes accessed | tf_op | source)
XLA Modules:
  0.0 434.8 jit_solution(13119818219933887852)
XLA Ops:
  1.5 3.7 collective-permute-start
  26.3 2.1 fusion.119
  30.5 2.2 fusion.125
  38.9 2.1 fusion.89
  43.1 2.1 fusion.95
  47.3 2.3 fusion.128
  55.6 13.9 %add_add_fusion.1 = f32[256,16,128]{0,2,1:T(8,128)} fusion(f32[256,16,128]{0,2,1:T(8,128)} %fusion.71, f32[256,16,128]{0,2,1:T(8,128)} %fusion.128, f32[256,16,128]{0,2,1:T(8,128)} %fusion.125, f32[256,16,128]{0,2,1:T(8,128)} %fusion.122, f32[256,16,128]{0,2,1:T(8,128)} %fusion.119, f32[256,16,128]{0,2,1:T(8,128)} %fusion.116, ...), kind=kOutput, calls=%fused_computation.52 | convolution fusion | flops 168099840 | bytes 45385216 | tf_op jit(solution)/shard_map/rgk,ko->rgo/dot_general | solution.py:62
  69.5 3.1 copy.57
  72.6 4.3 fusion.172
  76.9 38.6 %all_to_all.15 = bf16[32,8,2048]{2,1,0:T(8,128)(2,1)S(1)} all-to-all(bf16[32,8,2048]{2,1,0:T(8,128)(2,1)S(1)} %get-tuple-element.17), channel_id=1, replica_groups=mesh['visit'=32,'tile'=8] {'visit'}, dimensions={0} | all-to-all | bytes 2097152 | tf_op jit(solution)/shard_map/all_to_all | solution.py:103
  115.5 4.6 %all-to-all-start.1 = ((bf16[32,8,2048]{2,1,0:T(8,128)(2,1)}), bf16[32,8,2048]{2,1,0:T(8,128)(2,1)S(1)}, u32[]{:S(2)}, u32[]{:S(2)}) async-start(bf16[32,8,2048]{2,1,0:T(8,128)(2,1)} %get-tuple-element.16), calls=%async_computation.1 | async-start | bytes 2097152 | tf_op jit(solution)/shard_map/all_to_all | solution.py:104
  121.4 27.4 %all-to-all-done.1 = bf16[32,8,2048]{2,1,0:T(8,128)(2,1)S(1)} async-done(((bf16[32,8,2048]{2,1,0:T(8,128)(2,1)}), bf16[32,8,2048]{2,1,0:T(8,128)(2,1)S(1)}, u32[]{:S(2)}, u32[]{:S(2)}) %all-to-all-start.1) | async-done | bytes 1048608 | tf_op jit(solution)/shard_map/all_to_all | solution.py:104
  150.1 4.3 stack.2
  154.5 5.2 %all-to-all-start.2 = ((bf16[32,8,8,2048]{3,2,1,0:T(8,128)(2,1)}), bf16[32,8,8,2048]{3,2,1,0:T(8,128)(2,1)}, u32[]{:S(2)}, u32[]{:S(2)}) async-start(bf16[32,8,8,2048]{3,2,1,0:T(8,128)(2,1)} %stack.2), calls=%async_computation.2 | async-start | bytes 16777216 | tf_op jit(solution)/shard_map/all_to_all | solution.py:10
  162.7 2.2 fusion.354
  165.7 193.5 %all-to-all-done.2 = bf16[32,8,8,2048]{3,2,1,0:T(8,128)(2,1)} async-done(((bf16[32,8,8,2048]{3,2,1,0:T(8,128)(2,1)}), bf16[32,8,8,2048]{3,2,1,0:T(8,128)(2,1)}, u32[]{:S(2)}, u32[]{:S(2)}) %all-to-all-start.2) | async-done | bytes 8388640 | tf_op jit(solution)/shard_map/all_to_all | solution.py:10
  359.2 8.3 %copy.282 = bf16[32,8,8,2048]{3,2,0,1:T(8,128)(2,1)} copy(bf16[32,8,8,2048]{3,2,1,0:T(8,128)(2,1)} %all-to-all-done.2) | data formatting | bytes 16777216 | tf_op jit(solution)/shard_map/all_to_all | solution.py:10
  370.4 2.7 collective-permute-start.3
  386.9 2.1 fusion.32
  391.1 2.2 fusion.38
  403.7 2.1 fusion.56
  407.9 2.2 fusion.62
  410.0 2.3 fusion.65
  416.5 14.4 %add_add_fusion = f32[256,16,128]{0,2,1:T(8,128)} fusion(f32[256,16,128]{0,2,1:T(8,128)} %fusion.11, f32[256,16,128]{0,2,1:T(8,128)} %fusion.68, f32[256,16,128]{0,2,1:T(8,128)} %fusion.65, f32[256,16,128]{0,2,1:T(8,128)} %fusion.62, f32[256,16,128]{0,2,1:T(8,128)} %fusion.59, f32[256,16,128]{0,2,1:T(8,128)} %fusion.56, f32[256,16,128]{0,2,1:T(8,128)} %fusion.53, ...), kind=kOutput, calls=%fused_computation.49 | convolution fusion | flops 168099840 | bytes 45385216 | tf_op jit(solution)/shard_map/rgk,ko->rgo/dot_general | solution.py:62
  (151 shorter events, 82.3 us)
Async XLA Ops:
  0.6 159.0 %copy-start = (s32[32,1]{0,1:T(1,128)S(1)}, s32[32,1]{0,1:T(1,128)}, u32[]{:S(2)}) copy-start(s32[32,1]{0,1:T(1,128)} %param.21) | copy-start | bytes 388
  1.5 13.5 %collective-permute-start = (bf16[10,2048]{1,0:T(8,128)(2,1)S(1)}, bf16[10,2048]{1,0:T(8,128)(2,1)S(1)}, u32[]{:S(2)}, u32[]{:S(2)}) collective-permute-start(bf16[10,2048]{1,0:T(8,128)(2,1)S(1)} %get-tuple-element.18), channel_id=1, source_target_pairs={{0,1},{1,2},{2,3},{3,4},{4,5},{5,6},{6,7},{8,9},{9,10},{10,11},{11... | collective-permute-start | bytes 122888 | tf_op jit(solution)/shard_map/ppermute | solution.py:25
  5.2 9.8 %collective-permute-start.1 = (bf16[10,2048]{1,0:T(8,128)(2,1)S(1)}, bf16[10,2048]{1,0:T(8,128)(2,1)S(1)}, u32[]{:S(2)}, u32[]{:S(2)}) collective-permute-start(bf16[10,2048]{1,0:T(8,128)(2,1)S(1)} %get-tuple-element.19), channel_id=1, source_target_pairs={{1,0},{2,1},{3,2},{4,3},{5,4},{6,5},{7,6},{9,8},{10,9},{11,10},{12... | collective-permute-start | bytes 122888 | tf_op jit(solution)/shard_map/ppermute | solution.py:28
  8.8 2.6 copy-start.3
  11.4 3.7 copy-start.4
  26.3 2.1 copy-start.36
  30.5 2.2 copy-start.34
  38.9 2.1 copy-start.30
  43.1 2.1 copy-start.28
  47.3 2.3 copy-start.24
  69.5 3.1 copy-start.2
  76.9 43.3 %copy-start.42 = (s32[32,1]{0,1:T(1,128)S(1)}, s32[32,1]{0,1:T(1,128)}, u32[]{:S(2)}) copy-start(s32[32,1]{0,1:T(1,128)} %param.18) | copy-start | bytes 388
  115.5 33.2 %all-to-all-start.1 = ((bf16[32,8,2048]{2,1,0:T(8,128)(2,1)}), bf16[32,8,2048]{2,1,0:T(8,128)(2,1)S(1)}, u32[]{:S(2)}, u32[]{:S(2)}) async-start(bf16[32,8,2048]{2,1,0:T(8,128)(2,1)} %get-tuple-element.16), calls=%async_computation.1 | async-start | bytes 2097152 | tf_op jit(solution)/shard_map/all_to_all | solution.py:104
  154.5 204.8 %all-to-all-start.2 = ((bf16[32,8,8,2048]{3,2,1,0:T(8,128)(2,1)}), bf16[32,8,8,2048]{3,2,1,0:T(8,128)(2,1)}, u32[]{:S(2)}, u32[]{:S(2)}) async-start(bf16[32,8,8,2048]{3,2,1,0:T(8,128)(2,1)} %stack.2), calls=%async_computation.2 | async-start | bytes 16777216 | tf_op jit(solution)/shard_map/all_to_all | solution.py:10
  368.4 6.0 %collective-permute-start.2 = (bf16[10,2048]{1,0:T(8,128)(2,1)S(1)}, bf16[10,2048]{1,0:T(8,128)(2,1)S(1)}, u32[]{:S(2)}, u32[]{:S(2)}) collective-permute-start(bf16[10,2048]{1,0:T(8,128)(2,1)S(1)} %get-tuple-element.14), channel_id=1, source_target_pairs={{0,1},{1,2},{2,3},{3,4},{4,5},{5,6},{6,7},{8,9},{9,10},{10,11},{11... | collective-permute-start | bytes 122888 | tf_op jit(solution)/shard_map/ppermute | solution.py:25
  370.4 5.6 %collective-permute-start.3 = (bf16[10,2048]{1,0:T(8,128)(2,1)S(1)}, bf16[10,2048]{1,0:T(8,128)(2,1)S(1)}, u32[]{:S(2)}, u32[]{:S(2)}) collective-permute-start(bf16[10,2048]{1,0:T(8,128)(2,1)S(1)} %get-tuple-element.15), channel_id=1, source_target_pairs={{1,0},{2,1},{3,2},{4,3},{5,4},{6,5},{7,6},{9,8},{10,9},{11,10},{12... | collective-permute-start | bytes 122888 | tf_op jit(solution)/shard_map/ppermute | solution.py:28
  382.6 2.1 copy-start.22
  386.9 2.1 copy-start.20
  391.1 2.2 copy-start.18
  399.4 2.1 copy-start.14
  403.7 2.1 copy-start.12
  407.9 2.2 copy-start.10
  410.0 2.3 copy-start.9
  430.9 3.6 copy-start.1
  (25 other events, 46.9 us)
